TPU v7x, 512 devices: a whole 4x4x16 slice. The times are simulated.
512 devices in a mesh: layer: 2 (over core), latent: 32 (over z_hi, y, x), token: 8 (over z_lo).
Axes of the slice: x: 4, y: 4, z: 16 (z_hi: 2, z_lo: 8; z = z_hi * 8 + z_lo), core: 2. Of those that a mesh axis runs over, the one named last changes fastest.
Arguments:
- taps: bfloat16 [2, 1792, 3584], P('layer', 'token'), may hold values from -6 to 6
- token_ids: int32 [1792], P('token'), may hold values from 2 to 255999, as said below
- enc_weight: bfloat16 [2, 3584, 8192], P('layer', 'token', 'latent'), may hold values from -0.0625 to 0.0625
- enc_bias: float32 [8192], P('latent'), may hold values from -3 to 3
- dec_weight: bfloat16 [2, 3584, 8192], P('layer', 'token', 'latent'), as said below
- dec_bias: float32 [2, 3584], P('layer'), may hold values from -3 to 3
Outputs:
- enc_grad: bfloat16 [2, 3584, 8192], P('layer', 'token', 'latent')
- dec_grad: bfloat16 [2, 3584, 8192], P('layer', 'token', 'latent')
Inputs may be any that keep to these rules, and one draw needn't show every extreme that they name: `token_ids`: id 2 marks the beginning of a document and stands at position 0; all other ids are 3 or more. `dec_weight`: entries of order 8192^-0.5.
All inputs are finite; a program needn't handle non-finite values.
Results may differ from a plain program's by a relative error of at most 0.014.
Values may be sent and summed in bfloat16 or wider, within the bound.
A program may use at most 64 MiB of HBM per device.

v0:
```python
import math
import jax
import jax.numpy as jnp
from jax import lax
from jax.sharding import PartitionSpec as P

KNEE_WIDTH = 0.5
SPARSITY = 0.5
BEGIN_TOKEN = 2


def smooth_relu(preact):
    positive = jnp.maximum(preact, 0.0)
    return jnp.where(
        positive < KNEE_WIDTH, positive * positive / (2.0 * KNEE_WIDTH), positive - 0.5 * KNEE_WIDTH
    )


def relu_slope(preact):
    return jnp.clip(preact / KNEE_WIDTH, 0.0, 1.0)


def local(taps, token_ids, enc_weight, enc_bias, dec_weight, dec_bias):
    tap_rows = taps[0]
    tokens_dev = tap_rows.shape[0]
    loss_scale = 1.0 / math.sqrt(tokens_dev * lax.axis_size("token"))
    keep_mask = (token_ids != BEGIN_TOKEN).astype(jnp.float32)
    partial_pre = jnp.dot(
        tap_rows,
        lax.all_gather(enc_weight[0], "token", axis=0, tiled=True),
        preferred_element_type=jnp.float32,
    )
    preact = lax.psum(partial_pre, "layer") + enc_bias[None, :]
    features = smooth_relu(preact).astype(jnp.bfloat16)
    dec_full = lax.all_gather(dec_weight[0], "token", axis=0, tiled=True)
    rebuilt_part = lax.dot_general(
        features, dec_full, (((1,), (1,)), ((), ())), preferred_element_type=jnp.float32
    )
    rebuilt = lax.psum(rebuilt_part, "latent") + dec_bias[0][None, :]
    residue = (loss_scale * keep_mask[:, None] * (rebuilt - tap_rows.astype(jnp.float32))).astype(
        jnp.bfloat16
    )
    colnorm = jnp.sqrt(jnp.sum(jnp.square(dec_full.astype(jnp.float32)), axis=0) + 1e-06)
    back_part = jnp.dot(residue, dec_full, preferred_element_type=jnp.float32)
    feat_back, norm_total = lax.psum((back_part, colnorm), "layer")
    feat_grads = feat_back + loss_scale * SPARSITY * keep_mask[:, None] * norm_total[None, :]
    pre_grads = (feat_grads * relu_slope(preact)).astype(jnp.bfloat16)
    activity = jnp.sum(keep_mask[:, None] * features.astype(jnp.float32), axis=0)
    penalty_scale = loss_scale * SPARSITY * activity / colnorm
    product = lax.dot_general(
        residue, features, (((0,), (0,)), ((), ())), preferred_element_type=jnp.float32
    )
    dec_grad = lax.psum_scatter(
        (product + dec_full.astype(jnp.float32) * penalty_scale[None, :]).astype(jnp.bfloat16),
        "token",
        scatter_dimension=0,
        tiled=True,
    )
    enc_grad = lax.psum_scatter(
        lax.dot_general(
            tap_rows, pre_grads, (((0,), (0,)), ((), ())), preferred_element_type=jnp.float32
        ).astype(jnp.bfloat16),
        "token",
        scatter_dimension=0,
        tiled=True,
    )
    return (enc_grad[None], dec_grad[None])


def solution(mesh):
    placed = (
        P("layer", "token", None),
        P("token"),
        P("layer", "token", "latent"),
        P("latent"),
        P("layer", "token", "latent"),
        P("layer", None),
    )
    return jax.shard_map(
        local,
        mesh=mesh,
        in_specs=placed,
        out_specs=(P("layer", "token", "latent"), P("layer", "token", "latent")),
        check_vma=False,
    )
```

profile of v0, /device:TPU:6, one launch (start us, length us, event | category | flops | bytes accessed | tf_op | source)
XLA Modules:
  0.0 1122.9 jit_solution(13959128137853227899)
XLA Ops:
  7.2 0.0 all-gather.5.cloned.1.call-start
  7.2 0.7 all-gather.5.cloned.1.call-update
  7.9 0.0 copy-start.6
  7.9 0.0 copy-start.7
  7.9 0.0 all-reduce.4.cloned.1.call-start
  8.0 76.5 %all-gather.5.cloned.1.call-done = bf16[1,3584,256]{2,1,0:T(8,128)(2,1)} async-done(((bf16[1,448,256]{2,1,0:T(8,128)(2,1)}), bf16[1,3584,256]{2,1,0:T(8,128)(2,1)}) %all-gather.5.cloned.1.call-update) | async-done | bytes 1835024 | tf_op jit(solution)/shard_map/all_gather | solution.py:30
  84.5 3.3 fusion.7
  87.7 0.0 all-reduce.4.cloned.1.call-update
  87.7 0.0 all-gather.7.cloned.1.call-start
  87.8 0.7 all-gather.7.cloned.1.call-update
  88.5 0.0 all-reduce.6.cloned.1.call-start
  88.5 0.0 copy-done.6
  88.5 34.3 %all-reduce.4.cloned.1.call-done = f32[224,256]{1,0:T(8,128)} async-done(((f32[224,256]{1,0:T(8,128)}), f32[224,256]{1,0:T(8,128)}) %all-reduce.4.cloned.1.call-update) | async-done | bytes 229392 | tf_op jit(solution)/shard_map/psum | solution.py:33
  122.9 0.0 copy-done.7
  122.9 1.6 multiply_reduce_fusion
  124.5 71.8 %all-gather.7.cloned.1.call-done = bf16[1,3584,256]{2,1,0:T(8,128)(2,1)} async-done(((bf16[1,448,256]{2,1,0:T(8,128)(2,1)}), bf16[1,3584,256]{2,1,0:T(8,128)(2,1)}) %all-gather.7.cloned.1.call-update) | async-done | bytes 1835024 | tf_op jit(solution)/shard_map/all_gather | solution.py:35
  196.3 3.9 fusion.5
  200.2 0.0 all-reduce.6.cloned.1.call-update
  200.2 0.0 all-reduce.8.cloned.1.call-start
  200.3 0.6 copy-done.4
  200.9 0.6 reduce
  201.5 0.6 broadcast_select_fusion
  202.1 692.7 %all-reduce.6.cloned.1.call-done = f32[224,3584]{1,0:T(8,128)} async-done(((f32[224,3584]{1,0:T(8,128)}), f32[224,3584]{1,0:T(8,128)}) %all-reduce.6.cloned.1.call-update) | async-done | bytes 3211280 | tf_op jit(solution)/shard_map/psum | solution.py:39
  894.9 0.0 copy-done.1
  894.9 2.6 multiply_convert_fusion
  897.5 0.0 copy-start.2
  897.5 1.2 copy-done.2
  898.6 0.0 copy-done
  898.6 1.3 fusion.3
  899.9 0.0 all-reduce.8.cloned.1.call-update
  899.9 0.0 reduce-scatter.7.cloned.1.call-start
  900.0 0.0 copy-start.5
  900.0 0.5 fusion.2
  900.5 0.2 copy-done.5
  900.7 0.6 rsqrt_multiply_fusion
  901.2 3.1 psum.31
  904.4 60.8 %all-reduce.8.cloned.1.call-done = f32[224,256]{1,0:T(8,128)} async-done(((f32[224,256]{1,0:T(8,128)}), f32[224,256]{1,0:T(8,128)}) %all-reduce.8.cloned.1.call-update) | async-done | bytes 229392 | tf_op jit(solution)/shard_map/psum | solution.py:45
  965.2 3.1 fusion.1
  968.2 3.8 copy.10
  972.0 0.0 reduce-scatter.7.cloned.1.call-update
  972.1 0.0 reduce-scatter.5.cloned.1.call-start
  972.1 1.3 copy-done.3
  973.5 2.6 fusion
  976.1 0.0 reduce-scatter.5.cloned.1.call-update
  976.1 69.4 %reduce-scatter.7.cloned.1.call-done = bf16[448,256]{1,0:T(8,128)(2,1)} async-done(((bf16[3584,256]{1,0:T(8,128)(2,1)}), bf16[448,256]{1,0:T(8,128)(2,1)}) %reduce-scatter.7.cloned.1.call-update) | async-done | bytes 229392
  1045.5 1.1 copy.11
  1046.6 0.8 copy.9
  1047.4 68.7 %reduce-scatter.5.cloned.1.call-done = bf16[448,256]{1,0:T(8,128)(2,1)} async-done(((bf16[3584,256]{1,0:T(8,128)(2,1)}), bf16[448,256]{1,0:T(8,128)(2,1)}) %reduce-scatter.5.cloned.1.call-update) | async-done | bytes 229392 | tf_op jit(solution)/shard_map/reduce_scatter | solution.py:53
  (5 shorter events, 0.0 us)
Async XLA Ops:
  7.2 77.3 %all-gather.5.cloned.1.call-start = ((), (), s32[]{:S(2)}) async-start(), calls=%async_computation.6 | async-start | bytes 2064384 | tf_op jit(solution)/shard_map/all_gather | solution.py:30
  7.9 80.6 %copy-start.6 = (s32[224]{0:T(256)S(1)}, s32[224]{0:T(256)}, u32[]{:S(2)}) copy-start(s32[224]{0:T(256)} %param.7) | copy-start | bytes 2692
  7.9 115.0 %copy-start.7 = (f32[256]{0:T(256)S(1)}, f32[256]{0:T(256)}, u32[]{:S(2)}) copy-start(f32[256]{0:T(256)} %param.9) | copy-start | bytes 3076
  7.9 114.9 %all-reduce.4.cloned.1.call-start = ((), (), s32[]{:S(2)}) async-start(), calls=%async_computation.2 | async-start | bytes 458752 | tf_op jit(solution)/shard_map/psum | solution.py:33
  87.7 108.5 %all-gather.7.cloned.1.call-start = ((), (), s32[]{:S(2)}) async-start(), calls=%async_computation.7 | async-start | bytes 2064384 | tf_op jit(solution)/shard_map/all_gather | solution.py:35
  88.5 806.4 %all-reduce.6.cloned.1.call-start = ((), (), s32[]{:S(2)}) async-start(), calls=%async_computation.3 | async-start | bytes 6422528 | tf_op jit(solution)/shard_map/psum | solution.py:39
  200.2 0.7 copy-start.4
  200.2 694.7 %copy-start.1 = (bf16[1,224,3584]{2,1,0:T(8,128)(2,1)S(1)}, bf16[1,224,3584]{2,1,0:T(8,128)(2,1)}, u32[]{:S(2)}) copy-start(bf16[1,224,3584]{2,1,0:T(8,128)(2,1)} %param.6) | copy-start | bytes 4816900
  200.2 765.0 %all-reduce.8.cloned.1.call-start = ((), (), s32[]{:S(2)}) async-start(), calls=%async_computation.4 | async-start | bytes 458752 | tf_op jit(solution)/shard_map/psum | solution.py:45
  894.9 3.7 copy-start
  897.5 1.2 copy-start.2
  899.9 145.6 %reduce-scatter.7.cloned.1.call-start = ((), (), s32[]{:S(2)}) async-start(), calls=%async_computation.8 | async-start | bytes 2064384
  900.0 0.7 copy-start.5
  972.0 1.4 copy-start.3
  972.1 144.0 %reduce-scatter.5.cloned.1.call-start = ((), (), s32[]{:S(2)}) async-start(), calls=%async_computation.5 | async-start | bytes 2064384 | tf_op jit(solution)/shard_map/reduce_scatter | solution.py:53
Sparse Core Ops, SparseCore 0:
  10.1 74.3 all-gather.4
  87.9 34.9 all-reduce.3
  125.0 71.2 all-gather.6
  200.3 694.4 all-reduce.5
  900.0 65.0 all-reduce.7
  972.2 73.2 reduce-scatter.6
  1049.2 66.8 reduce-scatter.4
where the time goes:
time: 1120 us
  waiting for transfers between devices  1080 us (96%)
  between operations  14.2 us (1%)
  matrix products  14.1 us (1%)
    psum x1, waiting for transfers between devices, local(): rebuilt = lax.psum(rebuilt_part, 'latent') + dec_bias[0][None, :]  693 us
    all_gather x1, waiting for transfers between devices, local(): lax.all_gather(enc_weight[0], 'token', axis=0, tiled=True)  76.5 us
    all_gather x1, waiting for transfers between devices, local(): dec_full = lax.all_gather(dec_weight[0], 'token', axis=0, tiled=True)  71.8 us
    unnamed x8, waiting for transfers between devices  70.8 us
    reduce_scatter x1, waiting for transfers between devices, local(): lax.psum_scatter((product + dec_full.astype(jnp.float32) * penalty_scale[...  68.7 us
    psum x1, waiting for transfers between devices, local(): feat_back, norm_total = lax.psum((back_part, colnorm), 'layer')  60.8 us
    psum x1, waiting for transfers between devices, local(): preact = lax.psum(partial_pre, 'layer') + enc_bias[None, :]  34.3 us
  transfers between devices with their start and end apart: 7, of which 7 were waited for; matrix products, arithmetic and copies ran while one was open for 1% of the time, Pallas kernels for 0%

commit v1 on v0

--- a/solution.py
+++ b/solution.py
@@ -3,10 +3,15 @@
 import jax.numpy as jnp
 from jax import lax
 from jax.sharding import PartitionSpec as P
+from jax.lax import all_gather
 
 KNEE_WIDTH = 0.5
 SPARSITY = 0.5
 BEGIN_TOKEN = 2
+
+
+def _spread_series_all(my_tile, along_axis):
+    return jnp.sum(all_gather(my_tile, along_axis), axis=0)
 
 
 def smooth_relu(preact):
@@ -30,7 +35,7 @@
         lax.all_gather(enc_weight[0], "token", axis=0, tiled=True),
         preferred_element_type=jnp.float32,
     )
-    preact = lax.psum(partial_pre, "layer") + enc_bias[None, :]
+    preact = _spread_series_all(partial_pre, "layer") + enc_bias[None, :]
     features = smooth_relu(preact).astype(jnp.bfloat16)
     dec_full = lax.all_gather(dec_weight[0], "token", axis=0, tiled=True)
     rebuilt_part = lax.dot_general(

time: 1120 us -> 1080 us (0.964)
  waiting for transfers between devices: 1080 us -> 1030 us
    psum x1 -> x0, waiting for transfers between devices: 34.3 us -> none  [local(): preact = lax.psum(partial_pre, 'layer') + enc_bias[None, :]]
    unnamed x8 -> x7, waiting for transfers between devices: 70.8 us -> 70.6 us
  transfers between devices with their start and end apart: 7 -> 6, of which waited for: 7 -> 6; matrix products, arithmetic and copies ran while one was open for 1% -> 1% of each run, Pallas kernels for 0% -> 0%
where the time goes in v1:
time: 1080 us
  waiting for transfers between devices  1030 us (95%)
  between operations  14.2 us (1%)
  matrix products  13.4 us (1%)
    psum x1, waiting for transfers between devices, local(): rebuilt = lax.psum(rebuilt_part, 'latent') + dec_bias[0][None, :]  691 us
    all_gather x1, waiting for transfers between devices, local(): lax.all_gather(enc_weight[0], 'token', axis=0, tiled=True)  75.1 us
    unnamed x7, waiting for transfers between devices  70.6 us
    reduce_scatter x1, waiting for transfers between devices, local(): lax.psum_scatter((product + dec_full.astype(jnp.float32) * penalty_scale[...  68.5 us
    all_gather x1, waiting for transfers between devices, local(): dec_full = lax.all_gather(dec_weight[0], 'token', axis=0, tiled=True)  62.3 us
    psum x1, waiting for transfers between devices, local(): feat_back, norm_total = lax.psum((back_part, colnorm), 'layer')  60.8 us
  transfers between devices with their start and end apart: 6, of which 6 were waited for; matrix products, arithmetic and copies ran while one was open for 1% of the time, Pallas kernels for 0%

profile of v1, /device:TPU:6, one launch (start us, length us, event | category | flops | bytes accessed | tf_op | source)
XLA Modules:
  0.0 1077.0 jit_solution(7692575096615787914)
XLA Ops:
  7.2 0.0 all-gather.6.cloned.1.call-start
  7.2 0.7 all-gather.6.cloned.1.call-update
  7.9 0.0 all-gather.8.cloned.1.call-start
  7.9 0.7 all-gather.8.cloned.1.call-update
  8.6 0.0 all-reduce.3.cloned.1.call-start
  8.7 0.7 fusion.20
  9.4 0.0 copy-start.8
  9.4 75.1 %all-gather.6.cloned.1.call-done = bf16[1,3584,256]{2,1,0:T(8,128)(2,1)} async-done(((bf16[1,448,256]{2,1,0:T(8,128)(2,1)}), bf16[1,3584,256]{2,1,0:T(8,128)(2,1)}) %all-gather.6.cloned.1.call-update) | async-done | bytes 1835024 | tf_op jit(solution)/shard_map/all_gather | solution.py:35
  84.5 2.6 fusion.7
  87.0 2.1 all-gather.1
  89.2 0.0 copy-done.8
  89.2 0.0 copy-start.4
  89.2 0.7 multiply_reduce_fusion
  89.9 62.3 %all-gather.8.cloned.1.call-done = bf16[1,3584,256]{2,1,0:T(8,128)(2,1)} async-done(((bf16[1,448,256]{2,1,0:T(8,128)(2,1)}), bf16[1,3584,256]{2,1,0:T(8,128)(2,1)}) %all-gather.8.cloned.1.call-update) | async-done | bytes 1835024 | tf_op jit(solution)/shard_map/all_gather | solution.py:40
  152.2 0.0 copy-done.4
  152.2 3.9 fusion.5
  156.1 0.0 all-reduce.3.cloned.1.call-update
  156.2 0.0 all-reduce.5.cloned.1.call-start
  156.2 0.6 copy-done.5
  156.8 0.6 reduce
  157.5 0.0 copy-done.7
  157.5 0.6 broadcast_select_fusion
  158.1 691.3 %all-reduce.3.cloned.1.call-done = f32[224,3584]{1,0:T(8,128)} async-done(((f32[224,3584]{1,0:T(8,128)}), f32[224,3584]{1,0:T(8,128)}) %all-reduce.3.cloned.1.call-update) | async-done | bytes 3211280 | tf_op jit(solution)/shard_map/psum | solution.py:44
  849.4 0.0 copy-done.1
  849.4 2.6 multiply_convert_fusion
  852.0 0.0 copy-start.2
  852.0 1.1 copy-done.2
  853.1 0.0 copy-done
  853.1 1.3 fusion.3
  854.4 0.0 all-reduce.5.cloned.1.call-update
  854.4 0.0 reduce-scatter.7.cloned.1.call-start
  854.5 0.0 copy-start.6
  854.5 0.5 fusion.2
  855.0 0.1 copy-done.6
  855.1 0.6 rsqrt_multiply_fusion
  855.7 3.2 psum.23
  858.9 60.8 %all-reduce.5.cloned.1.call-done = f32[224,256]{1,0:T(8,128)} async-done(((f32[224,256]{1,0:T(8,128)}), f32[224,256]{1,0:T(8,128)}) %all-reduce.5.cloned.1.call-update) | async-done | bytes 229392 | tf_op jit(solution)/shard_map/psum | solution.py:50
  919.7 3.0 fusion.1
  922.7 3.8 copy.11
  926.5 0.0 reduce-scatter.7.cloned.1.call-update
  926.6 0.0 reduce-scatter.5.cloned.1.call-start
  926.6 1.3 copy-done.3
  928.0 2.6 fusion
  930.6 0.0 reduce-scatter.5.cloned.1.call-update
  930.6 69.1 %reduce-scatter.7.cloned.1.call-done = bf16[448,256]{1,0:T(8,128)(2,1)} async-done(((bf16[3584,256]{1,0:T(8,128)(2,1)}), bf16[448,256]{1,0:T(8,128)(2,1)}) %reduce-scatter.7.cloned.1.call-update) | async-done | bytes 229392
  999.7 1.1 copy.12
  1000.8 0.8 copy.10
  1001.6 68.5 %reduce-scatter.5.cloned.1.call-done = bf16[448,256]{1,0:T(8,128)(2,1)} async-done(((bf16[3584,256]{1,0:T(8,128)(2,1)}), bf16[448,256]{1,0:T(8,128)(2,1)}) %reduce-scatter.5.cloned.1.call-update) | async-done | bytes 229392 | tf_op jit(solution)/shard_map/reduce_scatter | solution.py:58
  (6 shorter events, 0.0 us)
Async XLA Ops:
  7.2 77.3 %all-gather.6.cloned.1.call-start = ((), (), s32[]{:S(2)}) async-start(), calls=%async_computation.5 | async-start | bytes 2064384 | tf_op jit(solution)/shard_map/all_gather | solution.py:35
  7.9 144.3 %all-gather.8.cloned.1.call-start = ((), (), s32[]{:S(2)}) async-start(), calls=%async_computation.6 | async-start | bytes 2064384 | tf_op jit(solution)/shard_map/all_gather | solution.py:40
  8.6 840.8 %all-reduce.3.cloned.1.call-start = ((), (), s32[]{:S(2)}) async-start(), calls=%async_computation.2 | async-start | bytes 6422528 | tf_op jit(solution)/shard_map/psum | solution.py:44
  9.4 79.8 %copy-start.8 = (f32[256]{0:T(256)S(1)}, f32[256]{0:T(256)}, u32[]{:S(2)}) copy-start(f32[256]{0:T(256)} %param.9) | copy-start | bytes 3076
  89.2 63.0 %copy-start.4 = (f32[224,256]{1,0:T(8,128)}, f32[224,256]{1,0:T(8,128)S(1)}, u32[]{:S(2)}) copy-start(f32[224,256]{1,0:T(8,128)S(1)} %reduce_sum.27) | copy-start | bytes 688132
  156.1 0.7 copy-start.5
  156.1 1.4 copy-start.7
  156.1 693.3 %copy-start.1 = (bf16[1,224,3584]{2,1,0:T(8,128)(2,1)S(1)}, bf16[1,224,3584]{2,1,0:T(8,128)(2,1)}, u32[]{:S(2)}) copy-start(bf16[1,224,3584]{2,1,0:T(8,128)(2,1)} %param.6) | copy-start | bytes 4816900
  156.2 763.5 %all-reduce.5.cloned.1.call-start = ((), (), s32[]{:S(2)}) async-start(), calls=%async_computation.3 | async-start | bytes 458752 | tf_op jit(solution)/shard_map/psum | solution.py:50
  849.4 3.7 copy-start
  852.0 1.2 copy-start.2
  854.4 145.3 %reduce-scatter.7.cloned.1.call-start = ((), (), s32[]{:S(2)}) async-start(), calls=%async_computation.7 | async-start | bytes 2064384
  854.5 0.6 copy-start.6
  926.5 1.4 copy-start.3
  926.6 143.6 %reduce-scatter.5.cloned.1.call-start = ((), (), s32[]{:S(2)}) async-start(), calls=%async_computation.4 | async-start | bytes 2064384 | tf_op jit(solution)/shard_map/reduce_scatter | solution.py:58
Sparse Core Ops, SparseCore 0:
  10.1 74.3 all-gather.5
  86.5 65.6 all-gather.7
  156.3 693.0 all-reduce.2
  854.6 65.0 all-reduce.4
  926.7 72.9 reduce-scatter.6
  1003.2 66.8 reduce-scatter.4
